TPU v7x, 256 devices: a whole 4x4x8 slice. The times are simulated.
256 devices in a mesh: row: 64 (over z, y, core), col: 4 (over x).
Axes of the slice: x: 4, y: 4, z: 8, core: 2. Of those that a mesh axis runs over, the one named last changes fastest.
Arguments:
- panel_col: float32 [131072, 256], P('row', 'col'), may hold values from -6 to 6
- look_cols: float32 [131072, 2048], P('row', 'col'), may hold values from -6 to 6
- sketch_map: float32 [256, 131072], P(None, 'row'), may hold values from -0.015625 to 0.015625
- upper_inv: float32 [256, 256], replicated, may hold values from -0.09375 to 0.09375
- lower_inv: float32 [256, 256], replicated, may hold values from -0.375 to 0.375
- pivots: int32 [256], replicated, may hold values from 256 to 131071, as said below
Outputs:
- l_panel: float32 [131072, 256], P('row', 'col')
- updated: float32 [131072, 2048], P('row', 'col')
- sketch: float32 [256, 256], P(None, 'col')
Inputs may be any that keep to these rules, and one draw needn't show every extreme that they name: `pivots`: distinct rows, none of them among the first 256.
All inputs are finite; a program needn't handle non-finite values.
Results may differ from a plain program's by a relative error of at most 0.000073.
Values sent between devices are 32-bit elements; how exact they have to be, the bound alone decides.
A program may use at most 64 MiB of HBM per device.

v0:
```python
import jax
import jax.numpy as jnp
from jax import lax
from jax.sharding import PartitionSpec as P

high_prec = lax.Precision.HIGHEST


def on_device(panel_col, look_cols, sketch_map, upper_inv, lower_inv, pivots):
    row_count = panel_col.shape[0]
    col_width = panel_col.shape[1]
    block_size = upper_inv.shape[0]
    col_index = lax.axis_index("col")
    row_index = lax.axis_index("row")
    first_row = row_index * row_count
    owned = (pivots >= first_row) & (pivots < first_row + row_count)
    local_idx = jnp.where(owned, pivots - first_row, 0)
    owned_mask = owned[:, None]
    panel_pick = jnp.where(owned_mask, panel_col[local_idx], 0.0)
    look_pick = jnp.where(owned_mask, look_cols[local_idx], 0.0)
    sketch_part = jnp.dot(
        sketch_map, panel_col, precision=high_prec, preferred_element_type=jnp.float32
    )
    on_root = row_index == 0
    panel_head = jnp.where(on_root, panel_col[:block_size], 0.0)
    look_head = jnp.where(on_root, look_cols[:block_size], 0.0)
    sketch, panel_piv, look_piv, panel_orig, look_orig = lax.psum(
        (sketch_part, panel_pick, look_pick, panel_head, look_head), "row"
    )
    target = jnp.where(owned, pivots - first_row, row_count)
    swapped_panel = panel_col.at[target].set(panel_orig, mode="drop")
    swapped_look = look_cols.at[target].set(look_orig, mode="drop")
    swapped_panel = jnp.where(on_root, swapped_panel.at[:block_size].set(panel_piv), swapped_panel)
    swapped_look = jnp.where(on_root, swapped_look.at[:block_size].set(look_piv), swapped_look)
    upper_tri = jnp.triu(upper_inv)
    lower_tri = jnp.tril(lower_inv, -1) + jnp.eye(block_size, dtype=jnp.float32)
    upper_rows = lax.dynamic_slice_in_dim(upper_tri, col_index * col_width, col_width, 0)
    partial_prod = jnp.dot(
        swapped_panel, upper_rows, precision=high_prec, preferred_element_type=jnp.float32
    )
    factor = lax.psum(partial_prod, "col")
    global_row = first_row + jnp.arange(row_count, dtype=jnp.int32)
    is_top = (global_row < block_size)[:, None]
    my_factor = lax.dynamic_slice_in_dim(factor, col_index * col_width, col_width, 1)
    l_panel = jnp.where(is_top, swapped_panel, my_factor)
    u_rows = jnp.dot(lower_tri, look_piv, precision=high_prec, preferred_element_type=jnp.float32)
    updated = swapped_look - jnp.dot(
        factor, u_rows, precision=high_prec, preferred_element_type=jnp.float32
    )
    updated = jnp.where(on_root, updated.at[:block_size].set(u_rows), updated)
    return (l_panel, updated, sketch)


def solution(mesh):
    placed = (P("row", "col"), P("row", "col"), P(None, "row"), P(), P(), P())
    return jax.shard_map(
        on_device,
        mesh=mesh,
        in_specs=placed,
        out_specs=(P("row", "col"), P("row", "col"), P(None, "col")),
        check_vma=False,
    )
```

profile of v0, /device:TPU:1, one launch (start us, length us, event | category | flops | bytes accessed | tf_op | source)
XLA Modules:
  0.0 307.5 jit_solution(13693479291795300407)
XLA Ops:
  7.2 0.0 all-reduce.6.cloned.1.call-start
  7.2 4.8 %copy.27 = f32[2048,512]{1,0:T(8,128)} copy(f32[2048,512]{1,0:T(8,128)} %param.13) | data formatting | bytes 8388608
  12.1 1.4 copy.10
  13.5 3.7 %fusion.14 = f32[256,64]{0,1:T(8,128)} fusion(f32[256,2048]{1,0:T(8,128)S(1)} %copy-done, f32[2048,64]{0,1:T(8,128)} %param.12), kind=kOutput, calls=%fused_computation.36 | convolution fusion | flops 402653184 | bytes 2686976 | tf_op jit(solution)/shard_map/dot_general | solution.py:21
  17.2 0.7 gather_fusion
  17.9 4.2 %gather_fusion.1 = f32[256,512]{1,0:T(8,128)} fusion(f32[2048,512]{1,0:T(8,128)} %copy.27, s32[1024]{0:T(1024)S(1)} %pad_clamp_fusion), kind=kCustom, calls=%fused_computation.1 | custom fusion | bytes 1049600 | tf_op jit(solution)/shard_map/gather | solution.py:20
  22.1 0.7 slice_select_fusion.4
  22.8 2.3 slice_select_fusion.2
  25.1 0.0 all-reduce.6.cloned.1.call-update
  25.1 0.0 all-reduce.4.cloned.1.call-start
  25.2 0.1 iota_compare_fusion.1
  25.3 190.4 %all-reduce.6.cloned.1.call-done = (f32[256,64]{1,0:T(8,128)}, f32[256,64]{1,0:T(8,128)}, f32[256,512]{1,0:T(8,128)}, f32[256,512]{1,0:T(8,128)}, f32[256,64]{0,1:T(8,128)}) async-done(((f32[256,64]{1,0:T(8,128)}, f32[256,64]{1,0:T(8,128)}, f32[256,512]{1,0:T(8,128)}, f32[256,512]{1,0:T(8,128)}, f32[256,64]{0,1:T(8,128)}), (f32[256,64]{1,0:T(8,128)}, f32[256,64]{1,0:T(8,128)}, f32[256,512]{1,0:T(8,128)}, ...) | async-done | bytes 1245200 | tf_op jit(solution)/shard_map/psum | solution.py:27
  215.7 1.9 scatter_fusion
  217.7 3.9 %fusion.8 = f32[2048,256]{1,0:T(8,128)} fusion(f32[2048,64]{1,0:T(8,128)S(1)} %fusion.6, f32[256,256]{1,0:T(8,128)} %param.15, s32[]{:T(128)S(6)} %select_n.87, pred[256,256]{1,0:T(32,128)(4,1)S(1)} %iota_compare_fusion.1), kind=kOutput, calls=%fused_computation.23 | convolution fusion | flops 402669568 | bytes 3227652 | tf_op jit(solution)/shard_map/dot_general | solution.py:38
  221.6 0.0 all-reduce.4.cloned.1.call-update
  221.7 6.1 %scatter_fusion.1 = f32[2048,512]{1,0:T(8,128)} fusion(f32[2048,512]{1,0:T(8,128)} %copy.27, s32[256]{0:T(256)S(1)} %get-tuple-element.48, f32[256,512]{1,0:T(8,128)} %get-tuple-element.44), kind=kCustom, calls=%fused_computation.3 | custom fusion | bytes 1573888 | tf_op jit(solution)/shard_map/scatter | solution.py:32
  227.8 2.5 fusion.2
  230.3 1.9 fusion.1
  232.2 53.3 %all-reduce.4.cloned.1.call-done = f32[2048,256]{1,0:T(8,128)} async-done(((f32[2048,256]{1,0:T(8,128)}), f32[2048,256]{1,0:T(8,128)}) %all-reduce.4.cloned.1.call-update) | async-done | bytes 2097168 | tf_op jit(solution)/shard_map/psum | solution.py:41
  285.5 8.7 %convolution_subtract_fusion = f32[2048,512]{1,0:T(8,128)} fusion(f32[2048,512]{1,0:T(8,128)} %fusion.1, f32[2048,256]{1,0:T(8,128)} %all-reduce.4.cloned.1.call-done, f32[256,512]{1,0:T(8,128)} %fusion.2), kind=kOutput, calls=%fused_computation.4 | convolution fusion | flops 3222274048 | bytes 11010048 | tf_op jit(solution)/shard_map/dot_general | solution.py:47
  294.1 1.9 fusion
  296.1 1.6 dynamic-slice_select_fusion
  297.7 2.3 copy.12
  300.0 0.6 copy.28
  (18 shorter events, 0.1 us)
Async XLA Ops:
  7.2 6.3 %copy-start = (f32[256,2048]{1,0:T(8,128)S(1)}, f32[256,2048]{1,0:T(8,128)}, u32[]{:S(2)}) copy-start(f32[256,2048]{1,0:T(8,128)} %param.14) | copy-start | bytes 6291460
  7.2 4.8 %copy-start.5 = (s32[256]{0:T(256)S(1)}, s32[256]{0:T(256)}, u32[]{:S(2)}) copy-start(s32[256]{0:T(256)} %param.17) | copy-start | bytes 3076
  7.2 208.5 %all-reduce.6.cloned.1.call-start = ((), (), s32[]{:S(2)}) async-start(), calls=%async_computation.1 | async-start | bytes 2752512 | tf_op jit(solution)/shard_map/psum | solution.py:27
  25.1 260.4 %all-reduce.4.cloned.1.call-start = ((), (), s32[]{:S(2)}) async-start(), calls=%async_computation | async-start | bytes 4194304 | tf_op jit(solution)/shard_map/psum | solution.py:41
  221.7 6.1 %copy-start.3 = (f32[256,256]{1,0:T(8,128)S(1)}, f32[256,256]{1,0:T(8,128)}, u32[]{:S(2)}) copy-start(f32[256,256]{1,0:T(8,128)} %param.16) | copy-start | bytes 786436
  285.5 8.7 %copy-start.2 = (f32[256,512]{1,0:T(8,128)S(1)}, f32[256,512]{1,0:T(8,128)}, u32[]{:S(2)}) copy-start(f32[256,512]{1,0:T(8,128)} %fusion.2) | copy-start | bytes 1572868
  285.5 10.6 %copy-start.1 = (f32[2048,256]{1,0:T(8,128)S(1)}, f32[2048,256]{1,0:T(8,128)}, u32[]{:S(2)}) copy-start(f32[2048,256]{1,0:T(8,128)} %all-reduce.4.cloned.1.call-done) | copy-start | bytes 6291460
  294.1 5.9 %copy-start.4 = (f32[256,64]{0,1:T(8,128)S(1)}, f32[256,64]{0,1:T(8,128)}, u32[]{:S(2)}) copy-start(f32[256,64]{0,1:T(8,128)} %get-tuple-element.55) | copy-start | bytes 196612
Sparse Core Ops, SparseCore 0:
  25.2 190.4 all-reduce.5
  221.8 63.6 all-reduce.3
where the time goes:
time: 308 us; the launch traced here: 307 us
  waiting for transfers between devices  244 us (79%)
  local copies, waits for them, and re-layouts  22.1 us (7%)
  matrix products  18.8 us (6%)
  between operations  14.2 us (5%)
  other arithmetic  8.61 us (3%)
    psum x1, waiting for transfers between devices, on_device(): lax.psum((sketch_part, panel_pick, look_pick, panel_head, look_head), 'row')  190 us
    psum x1, waiting for transfers between devices, on_device(): factor = lax.psum(partial_prod, 'col')  53.3 us
    unnamed x16, local copies, waits for them, and re-layouts  9.15 us
    dot_general x1, matrix products, on_device(): jnp.dot(factor, u_rows, precision=high_prec, preferred_element_type=jnp.f...  8.65 us
  transfers between devices with their start and end apart: 2, of which 2 were waited for; matrix products, arithmetic and copies ran while one was open for 3% of the time, Pallas kernels for 0%

commit v1 on v0

--- a/solution.py
+++ b/solution.py
@@ -38,7 +38,7 @@
     partial_prod = jnp.dot(
         swapped_panel, upper_rows, precision=high_prec, preferred_element_type=jnp.float32
     )
-    factor = lax.psum(partial_prod, "col")
+    factor = jnp.sum(lax.all_gather(partial_prod, "col"), axis=0)
     global_row = first_row + jnp.arange(row_count, dtype=jnp.int32)
     is_top = (global_row < block_size)[:, None]
     my_factor = lax.dynamic_slice_in_dim(factor, col_index * col_width, col_width, 1)

time: 308 us -> 335 us (1.088)
  waiting for transfers between devices: 244 us -> 266 us
  other arithmetic: 8.61 us -> 14.1 us
    all_gather x0 -> x1, waiting for transfers between devices: none -> 75.2 us  [on_device(): factor = jnp.sum(lax.all_gather(partial_prod, 'col'), axis=0)]
    psum x1 -> x0, waiting for transfers between devices: 53.3 us -> none  [on_device(): factor = lax.psum(partial_prod, 'col')]
    reduce_sum x0 -> x1, other arithmetic: none -> 5.56 us  [on_device(): factor = jnp.sum(lax.all_gather(partial_prod, 'col'), axis=0)]
where the time goes in v1:
time: 335 us
  waiting for transfers between devices  266 us (79%)
  local copies, waits for them, and re-layouts  22.1 us (7%)
  matrix products  18.8 us (6%)
  other arithmetic  14.1 us (4%)
  between operations  14.1 us (4%)
    psum x1, waiting for transfers between devices, on_device(): lax.psum((sketch_part, panel_pick, look_pick, panel_head, look_head), 'row')  190 us
    all_gather x1, waiting for transfers between devices, on_device(): factor = jnp.sum(lax.all_gather(partial_prod, 'col'), axis=0)  75.2 us
    unnamed x16, local copies, waits for them, and re-layouts  9.15 us
    dot_general x1, matrix products, on_device(): jnp.dot(factor, u_rows, precision=high_prec, preferred_element_type=jnp.f...  8.65 us
  transfers between devices with their start and end apart: 2, of which 2 were waited for; matrix products, arithmetic and copies ran while one was open for 3% of the time, Pallas kernels for 0%

profile of v1, /device:TPU:1, one launch (start us, length us, event | category | flops | bytes accessed | tf_op | source)
XLA Modules:
  0.0 334.9 jit_solution(14925472281126796338)
XLA Ops:
  7.2 0.0 all-reduce.3.cloned.1.call-start
  7.2 4.8 %copy.26 = f32[2048,512]{1,0:T(8,128)} copy(f32[2048,512]{1,0:T(8,128)} %param.13) | data formatting | bytes 8388608
  12.1 1.4 copy.10
  13.4 4.2 %gather_fusion.1 = f32[256,512]{1,0:T(8,128)} fusion(f32[2048,512]{1,0:T(8,128)} %copy.26, s32[1024]{0:T(1024)S(1)} %pad_clamp_fusion), kind=kCustom, calls=%fused_computation.1 | custom fusion | bytes 1049600 | tf_op jit(solution)/shard_map/gather | solution.py:20
  17.6 0.7 gather_fusion
  18.3 2.2 slice_select_fusion.2
  20.6 0.7 slice_select_fusion.4
  21.3 3.7 %fusion.14 = f32[256,64]{0,1:T(8,128)} fusion(f32[256,2048]{1,0:T(8,128)S(1)} %copy-done, f32[2048,64]{0,1:T(8,128)} %param.12), kind=kOutput, calls=%fused_computation.36 | convolution fusion | flops 402653184 | bytes 2686976 | tf_op jit(solution)/shard_map/dot_general | solution.py:21
  25.0 0.0 all-reduce.3.cloned.1.call-update
  25.0 0.0 all-gather.3.cloned.1.call-start
  25.1 0.1 iota_compare_fusion.1
  25.2 190.4 %all-reduce.3.cloned.1.call-done = (f32[256,64]{1,0:T(8,128)}, f32[256,64]{1,0:T(8,128)}, f32[256,512]{1,0:T(8,128)}, f32[256,512]{1,0:T(8,128)}, f32[256,64]{0,1:T(8,128)}) async-done(((f32[256,64]{1,0:T(8,128)}, f32[256,64]{1,0:T(8,128)}, f32[256,512]{1,0:T(8,128)}, f32[256,512]{1,0:T(8,128)}, f32[256,64]{0,1:T(8,128)}), (f32[256,64]{1,0:T(8,128)}, f32[256,64]{1,0:T(8,128)}, f32[256,512]{1,0:T(8,128)}, ...) | async-done | bytes 1245200 | tf_op jit(solution)/shard_map/psum | solution.py:27
  215.6 1.9 scatter_fusion
  217.6 4.0 %fusion.8 = f32[2048,256]{1,0:T(8,128)} fusion(f32[2048,64]{1,0:T(8,128)S(1)} %fusion.6, f32[256,256]{1,0:T(8,128)} %param.15, s32[]{:T(128)S(6)} %select_n.87, pred[256,256]{1,0:T(32,128)(4,1)S(1)} %iota_compare_fusion.1), kind=kOutput, calls=%fused_computation.23 | convolution fusion | flops 402669568 | bytes 3227652 | tf_op jit(solution)/shard_map/dot_general | solution.py:38
  221.6 6.1 %scatter_fusion.1 = f32[2048,512]{1,0:T(8,128)} fusion(f32[2048,512]{1,0:T(8,128)} %copy.26, s32[256]{0:T(256)S(1)} %get-tuple-element.48, f32[256,512]{1,0:T(8,128)} %get-tuple-element.44), kind=kCustom, calls=%fused_computation.3 | custom fusion | bytes 1573888 | tf_op jit(solution)/shard_map/scatter | solution.py:32
  227.8 2.5 fusion.2
  230.3 1.9 fusion.1
  232.2 75.2 %all-gather.3.cloned.1.call-done = f32[8192,256]{1,0:T(8,128)} async-done(((f32[2048,256]{1,0:T(8,128)}), f32[8192,256]{1,0:T(8,128)}) %all-gather.3.cloned.1.call-update) | async-done | bytes 8388624 | tf_op jit(solution)/shard_map/all_gather | solution.py:41
  307.4 5.6 %reduce_sum.9 = f32[2048,256]{1,0:T(8,128)} reduce(f32[4,2048,256]{2,1,0:T(8,128)} %bitcast.7, f32[]{:T(128)} %constant.94.clone.1), dimensions={0}, to_apply=%region_3.4 | reduce | flops 1572864 | bytes 10485764 | tf_op jit(solution)/shard_map/reduce_sum | solution.py:41
  312.9 8.6 %convolution_subtract_fusion = f32[2048,512]{1,0:T(8,128)} fusion(f32[2048,512]{1,0:T(8,128)} %fusion.1, f32[2048,256]{1,0:T(8,128)} %reduce_sum.9, f32[256,512]{1,0:T(8,128)} %fusion.2), kind=kOutput, calls=%fused_computation.4 | convolution fusion | flops 3222274048 | bytes 11010048 | tf_op jit(solution)/shard_map/dot_general | solution.py:47
  321.6 1.9 fusion
  323.5 1.6 dynamic-slice_select_fusion
  325.1 2.3 copy.12
  327.4 0.6 copy.27
  (19 shorter events, 0.1 us)
Async XLA Ops:
  7.2 14.1 %copy-start = (f32[256,2048]{1,0:T(8,128)S(1)}, f32[256,2048]{1,0:T(8,128)}, u32[]{:S(2)}) copy-start(f32[256,2048]{1,0:T(8,128)} %param.14) | copy-start | bytes 6291460
  7.2 4.8 %copy-start.5 = (s32[256]{0:T(256)S(1)}, s32[256]{0:T(256)}, u32[]{:S(2)}) copy-start(s32[256]{0:T(256)} %param.17) | copy-start | bytes 3076
  7.2 208.5 %all-reduce.3.cloned.1.call-start = ((), (), s32[]{:S(2)}) async-start(), calls=%async_computation.1 | async-start | bytes 2752512 | tf_op jit(solution)/shard_map/psum | solution.py:27
  25.0 282.3 %all-gather.3.cloned.1.call-start = ((), (), s32[]{:S(2)}) async-start(), calls=%async_computation | async-start | bytes 10485760 | tf_op jit(solution)/shard_map/all_gather | solution.py:41
  221.6 6.1 %copy-start.3 = (f32[256,256]{1,0:T(8,128)S(1)}, f32[256,256]{1,0:T(8,128)}, u32[]{:S(2)}) copy-start(f32[256,256]{1,0:T(8,128)} %param.16) | copy-start | bytes 786436
  312.9 8.7 %copy-start.2 = (f32[256,512]{1,0:T(8,128)S(1)}, f32[256,512]{1,0:T(8,128)}, u32[]{:S(2)}) copy-start(f32[256,512]{1,0:T(8,128)} %fusion.2) | copy-start | bytes 1572868
  312.9 10.6 %copy-start.1 = (f32[2048,256]{1,0:T(8,128)S(1)}, f32[2048,256]{1,0:T(8,128)}, u32[]{:S(2)}) copy-start(f32[2048,256]{1,0:T(8,128)} %reduce_sum.9) | copy-start | bytes 6291460
  321.6 5.9 %copy-start.4 = (f32[256,64]{0,1:T(8,128)S(1)}, f32[256,64]{0,1:T(8,128)}, u32[]{:S(2)}) copy-start(f32[256,64]{0,1:T(8,128)} %get-tuple-element.55) | copy-start | bytes 196612
Sparse Core Ops, SparseCore 0:
  25.2 190.4 all-reduce.2
  221.7 85.5 all-gather.2
